TPU v7x, 32 devices: a whole 2x2x4 slice. The times are simulated.
32 devices in a mesh: dp: 16 (over z, x, core), tensor: 2 (over y).
Axes of the slice: x: 2, y: 2, z: 4, core: 2. Of those that a mesh axis runs over, the one named last changes fastest.
Arguments:
- tokens: bfloat16 [16, 1376, 1024], P('dp', 'tensor'), may hold values from -16 to 16
- cotangent: bfloat16 [16, 1376, 1024], P('dp', 'tensor'), may hold values from -6 to 6
- lengths: int32 [16], P('dp'), may hold values from 0 to 1370, as said below
- adapter_ids: int32 [16], P('dp'), may hold values from 0 to 7
- gain_one: float32 [1024], replicated, may hold values from 0.25 to 1.75
- gain_two: float32 [1024], replicated, may hold values from 0.25 to 1.75
- scale_one: float32 [1024], replicated, may hold values from 0.5 to 2
- scale_two: float32 [1024], replicated, may hold values from 0.5 to 2
- w_qkv: bfloat16 [1024, 3, 1024], P(None, None, 'tensor'), may hold values from -0.1875 to 0.1875
- w_out: bfloat16 [1024, 1024], P('tensor'), may hold values from -1 to 1
- w_up: bfloat16 [1024, 4096], P(None, 'tensor'), may hold values from -0.1875 to 0.1875
- w_down: bfloat16 [4096, 1024], P('tensor'), may hold values from -0.09375 to 0.09375
- qkv_a: bfloat16 [8, 16, 1024], replicated, may hold values from -0.1875 to 0.1875
- qkv_b: bfloat16 [8, 3, 1024, 16], P(None, None, 'tensor'), may hold values from -1.5 to 1.5
- out_a: bfloat16 [8, 16, 1024], P(None, None, 'tensor'), may hold values from -1 to 1
- out_b: bfloat16 [8, 1024, 16], replicated, may hold values from -1.5 to 1.5
- up_a: bfloat16 [8, 16, 1024], replicated, may hold values from -0.1875 to 0.1875
- up_b: bfloat16 [8, 4096, 16], P(None, 'tensor'), may hold values from -1.5 to 1.5
- down_a: bfloat16 [8, 16, 4096], P(None, None, 'tensor'), may hold values from -0.09375 to 0.09375
- down_b: bfloat16 [8, 1024, 16], replicated, may hold values from -1.5 to 1.5
Outputs:
- layer_out: bfloat16 [16, 1376, 1024], P('dp', 'tensor')
- grad_tokens: float32 [16, 1376, 1024], P('dp', 'tensor')
- grad_qkv_a: float32 [8, 16, 1024], replicated
- grad_qkv_b: float32 [8, 3, 1024, 16], P(None, None, 'tensor')
- grad_out_a: float32 [8, 16, 1024], P(None, None, 'tensor')
- grad_out_b: float32 [8, 1024, 16], replicated
- grad_up_a: float32 [8, 16, 1024], replicated
- grad_up_b: float32 [8, 4096, 16], P(None, 'tensor')
- grad_down_a: float32 [8, 16, 4096], P(None, None, 'tensor')
- grad_down_b: float32 [8, 1024, 16], replicated
Inputs may be any that keep to these rules, and one draw needn't show every extreme that they name: `lengths`: slots g * 1 to g + 1 - 1 belong to group g of the dp axis; the first c of them hold images, with c from (2) // 2 to 1, each of 685 to 1370 valid tokens, and the others are empty with length 0.
All inputs are finite; a program needn't handle non-finite values.
Results may differ from a plain program's by a relative error of at most 0.014.
The roundings to bfloat16 on the way count: a program that leaves them out, or rounds other values in their place, can miss the bound.
Values may be sent and summed in bfloat16 or wider, within the bound.
No kernel may reach another device: no remote copies, remote signals or barrier semaphores. Data moves between devices by JAX's collectives and lax.ppermute only.
A program may use at most 384 MiB of HBM per device.

v0:
```python
import jax
import jax.numpy as jnp
from jax import lax
from jax.sharding import PartitionSpec as P

HD = 64
ADAPTERS = 8
epsilon = 1e-06
masked_score = -1e30
HIGHEST = lax.Precision.HIGHEST


def product(form, left, right):
    return jnp.einsum(form, left, right, preferred_element_type=jnp.float32)


def precise(form, left, right):
    return jnp.einsum(form, left.astype(jnp.float32), right.astype(jnp.float32), precision=HIGHEST)


def select_rows(onehot, table):
    return product("sn,n...->s...", onehot, table).astype(table.dtype)


def norm_rows(values, gain_vec):
    average = jnp.mean(values, axis=-1, keepdims=True)
    centred = values - average
    variance = jnp.mean(centred * centred, axis=-1, keepdims=True)
    return centred * lax.rsqrt(variance + epsilon) * gain_vec


def norm_back(values, gain_vec, grad_normed):
    normed, pullback = jax.vjp(lambda rows: norm_rows(rows, gain_vec), values)
    return pullback(grad_normed)[0]


def gelu_slope(values):
    return (
        0.5 * (1.0 + lax.erf(values * 0.7071067811865476))
        + values * jnp.exp(-0.5 * values * values) * 0.3989422804014327
    )


def ffn_forward(rows_low, up_mat, down_mat, up_a_sel, up_b_sel, down_a_sel, down_b_sel):
    rank_up = product("std,srd->str", rows_low, up_a_sel).astype(jnp.bfloat16)
    preact = product("std,dh->sth", rows_low, up_mat) + product("str,shr->sth", rank_up, up_b_sel)
    hidden = jax.nn.gelu(preact, approximate=False).astype(jnp.bfloat16)
    rank_down = product("sth,srh->str", hidden, down_a_sel)
    terms = product("sth,hd->std", hidden, down_mat) + precise(
        "str,sdr->std", rank_down, down_b_sel
    )
    return (rank_up, preact, hidden, rank_down, terms)


def ffn_backward(
    rows_low,
    grad_rows,
    up_mat,
    down_mat,
    up_a_sel,
    up_b_sel,
    down_a_sel,
    down_b_sel,
    rank_up,
    preact,
    hidden,
    rank_down,
):
    grad_rank_down = product("std,sdr->str", grad_rows, down_b_sel).astype(jnp.bfloat16)
    grad_hidden = product("std,hd->sth", grad_rows, down_mat) + product(
        "str,srh->sth", grad_rank_down, down_a_sel
    )
    grad_preact = (grad_hidden * gelu_slope(preact)).astype(jnp.bfloat16)
    grad_up_b = product("sth,str->shr", grad_preact, rank_up)
    grad_rank_up = product("sth,shr->str", grad_preact, up_b_sel)
    grad_rows_in = product("sth,dh->std", grad_preact, up_mat) + precise(
        "str,srd->std", grad_rank_up, up_a_sel
    )
    grad_up_a = precise("str,std->srd", grad_rank_up, rows_low)
    grad_down_a = product("str,sth->srh", grad_rank_down, hidden)
    grad_down_b = precise("std,str->sdr", grad_rows, rank_down)
    return (grad_rows_in, (grad_up_a, grad_up_b, grad_down_a, grad_down_b))


def body(
    tokens,
    cotangent,
    lengths,
    adapter_ids,
    gain_one,
    gain_two,
    scale_one,
    scale_two,
    w_qkv,
    w_out,
    w_up,
    w_down,
    qkv_a,
    qkv_b,
    out_a,
    out_b,
    up_a,
    up_b,
    down_a,
    down_b,
):
    shard_rows = tokens.shape[1]
    seq_len = shard_rows * lax.axis_size("tensor")
    heads_local = w_qkv.shape[2] // HD
    scale_attn = HD ** (-0.5)
    first_row = lax.axis_index("tensor") * shard_rows
    positions = jnp.arange(seq_len, dtype=jnp.int32)
    key_valid = positions[None, :] < jnp.maximum(lengths, 1)[:, None]
    local_rows = first_row + jnp.arange(shard_rows, dtype=jnp.int32)
    row_valid = (local_rows[None, :] < lengths[:, None]).astype(jnp.float32)[:, :, None]
    adapters = jnp.arange(ADAPTERS, dtype=jnp.int32)
    onehot = (adapter_ids[:, None] == adapters[None, :]).astype(jnp.bfloat16)
    qkv_a_sel = select_rows(onehot, qkv_a)
    qkv_b_sel = select_rows(onehot, qkv_b)
    out_a_sel = select_rows(onehot, out_a)
    out_b_sel = select_rows(onehot, out_b)
    up_a_sel = select_rows(onehot, up_a)
    down_b_sel = select_rows(onehot, down_b)
    inputs = tokens.astype(jnp.float32)
    normed_one = norm_rows(inputs, gain_one).astype(jnp.bfloat16)
    full_one = lax.all_gather(normed_one, "tensor", axis=1, tiled=True)
    rank_qkv = product("std,srd->str", full_one, qkv_a_sel).astype(jnp.bfloat16)
    projected = (
        product("std,dcf->sctf", full_one, w_qkv) + product("str,scfr->sctf", rank_qkv, qkv_b_sel)
    ).astype(jnp.bfloat16)

    def split_heads(rows):
        return rows.reshape(seq_len, heads_local, HD)

    def masked_scores(queries, keyrows, valid_keys):
        scores = product("qhe,khe->hqk", queries, keyrows) * scale_attn
        return jnp.where(valid_keys[None, None, :], scores, masked_score)

    def attend(slot_items):
        slot_block, valid_keys = slot_items
        queries = split_heads(slot_block[0])
        keyrows = split_heads(slot_block[1])
        values = split_heads(slot_block[2])
        scores = masked_scores(queries, keyrows, valid_keys)
        row_max = jnp.max(scores, axis=-1, keepdims=True)
        exponent = jnp.exp(scores - row_max)
        row_total = jnp.sum(exponent, axis=-1, keepdims=True)
        soft_low = (exponent / row_total).astype(jnp.bfloat16)
        mixed_rows = (
            product("hqk,khe->qhe", soft_low, values).astype(jnp.bfloat16).reshape(seq_len, -1)
        )
        return (mixed_rows, (row_max + jnp.log(row_total))[:, :, 0])

    mixed, log_total = lax.map(attend, (projected, key_valid))
    rank_out = product("stf,srf->str", mixed, out_a_sel)
    attn_terms = product("stf,fd->std", mixed, w_out) + precise("str,sdr->std", rank_out, out_b_sel)
    attn_branch = lax.psum_scatter(attn_terms, "tensor", scatter_dimension=1, tiled=True)
    residual = inputs + scale_one * attn_branch
    normed_two = norm_rows(residual, gain_two).astype(jnp.bfloat16)
    up_mat, down_mat, up_b_all, down_a_all = (
        lax.all_gather(w_up, "tensor", axis=1, tiled=True),
        lax.all_gather(w_down, "tensor", axis=0, tiled=True),
        lax.all_gather(up_b, "tensor", axis=1, tiled=True),
        lax.all_gather(down_a, "tensor", axis=2, tiled=True),
    )
    up_b_sel = select_rows(onehot, up_b_all)
    down_a_sel = select_rows(onehot, down_a_all)
    rank_up, preact, hidden, rank_down, ffn_terms = ffn_forward(
        normed_two, up_mat, down_mat, up_a_sel, up_b_sel, down_a_sel, down_b_sel
    )
    layer_out = ((residual + scale_two * ffn_terms) * row_valid).astype(jnp.bfloat16)
    grad_out = cotangent.astype(jnp.float32) * row_valid
    grad_mlp = (scale_two * grad_out).astype(jnp.bfloat16)
    ffn_grad_in, ffn_grads = ffn_backward(
        normed_two,
        grad_mlp,
        up_mat,
        down_mat,
        up_a_sel,
        up_b_sel,
        down_a_sel,
        down_b_sel,
        rank_up,
        preact,
        hidden,
        rank_down,
    )
    grad_residual = grad_out + norm_back(residual, gain_two, ffn_grad_in)
    grad_attn = (scale_one * grad_residual).astype(jnp.bfloat16)
    full_grad_attn = lax.all_gather(grad_attn, "tensor", axis=1, tiled=True)
    grad_rank_out = product("std,sdr->str", full_grad_attn, out_b_sel).astype(jnp.bfloat16)
    grad_mixed = (
        product("std,fd->stf", full_grad_attn, w_out)
        + product("str,srf->stf", grad_rank_out, out_a_sel)
    ).astype(jnp.bfloat16)
    grad_out_a = product("str,stf->srf", grad_rank_out, mixed)
    grad_out_b = precise("std,str->sdr", full_grad_attn, rank_out)

    def attend_back(slot_items):
        slot_block, valid_keys, log_rows, grad_rows = slot_items
        queries = split_heads(slot_block[0])
        keyrows = split_heads(slot_block[1])
        values = split_heads(slot_block[2])
        scores = masked_scores(queries, keyrows, valid_keys)
        soft = jnp.exp(scores - log_rows[:, :, None])
        soft_low = soft.astype(jnp.bfloat16)
        grad_heads = split_heads(grad_rows)
        grad_soft = product("qhe,khe->hqk", grad_heads, values)
        grad_values = product("hqk,qhe->khe", soft_low, grad_heads)
        grad_scores = (
            soft * (grad_soft - jnp.sum(soft * grad_soft, axis=-1, keepdims=True))
        ).astype(jnp.bfloat16)
        grad_queries = product("hqk,khe->qhe", grad_scores, keyrows) * scale_attn
        grad_keys = product("hqk,qhe->khe", grad_scores, queries) * scale_attn
        return (
            jnp.stack([grad_queries, grad_keys, grad_values])
            .reshape(3, seq_len, -1)
            .astype(jnp.bfloat16)
        )

    grad_projected = lax.map(attend_back, (projected, key_valid, log_total, grad_mixed))
    grad_qkv_b = product("sctf,str->scfr", grad_projected, rank_qkv)
    grad_rank_qkv = product("sctf,scfr->str", grad_projected, qkv_b_sel)
    grad_one_terms = product("sctf,dcf->std", grad_projected, w_qkv) + precise(
        "str,srd->std", grad_rank_qkv, qkv_a_sel
    )
    grad_qkv_a = precise("str,std->srd", grad_rank_qkv, full_one)
    grad_normed_one = lax.psum_scatter(grad_one_terms, "tensor", scatter_dimension=1, tiled=True)
    grad_tokens = grad_residual + norm_back(inputs, gain_one, grad_normed_one)
    onehot_wide = onehot.astype(jnp.float32)

    def stack_slots(slot_grads):
        return jnp.einsum("sn,s...->n...", onehot_wide, slot_grads, precision=HIGHEST)

    grad_up_a, grad_up_b, grad_down_a, grad_down_b = ffn_grads
    sum_qkv_b, sum_out_a = lax.psum((stack_slots(grad_qkv_b), stack_slots(grad_out_a)), "dp")
    joint_sums = lax.psum(
        (
            stack_slots(grad_qkv_a),
            stack_slots(grad_out_b),
            stack_slots(grad_up_a),
            stack_slots(grad_up_b),
            stack_slots(grad_down_a),
            stack_slots(grad_down_b),
        ),
        ("dp", "tensor"),
    )
    sum_qkv_a, sum_out_b, sum_up_a, up_b_whole, down_a_whole, sum_down_b = joint_sums
    width_local = w_up.shape[1]
    first_col = lax.axis_index("tensor") * width_local
    sum_up_b = lax.dynamic_slice_in_dim(up_b_whole, first_col, width_local, 1)
    sum_down_a = lax.dynamic_slice_in_dim(down_a_whole, first_col, width_local, 2)
    return (
        layer_out,
        grad_tokens,
        sum_qkv_a,
        sum_qkv_b,
        sum_out_a,
        sum_out_b,
        sum_up_a,
        sum_up_b,
        sum_down_a,
        sum_down_b,
    )


def solution(mesh):
    return jax.shard_map(
        body,
        mesh=mesh,
        in_specs=(
            P("dp", "tensor", None),
            P("dp", "tensor", None),
            P("dp"),
            P("dp"),
            P(),
            P(),
            P(),
            P(),
            P(None, None, "tensor"),
            P("tensor", None),
            P(None, "tensor"),
            P("tensor", None),
            P(),
            P(None, None, "tensor", None),
            P(None, None, "tensor"),
            P(),
            P(),
            P(None, "tensor", None),
            P(None, None, "tensor"),
            P(),
        ),
        out_specs=(
            P("dp", "tensor", None),
            P("dp", "tensor", None),
            P(),
            P(None, None, "tensor", None),
            P(None, None, "tensor"),
            P(),
            P(),
            P(None, "tensor", None),
            P(None, None, "tensor"),
            P(),
        ),
        check_vma=False,
    )
```

profile of v0, /device:TPU:0, one launch (start us, length us, event | category | flops | bytes accessed | tf_op | source)
XLA Modules:
  0.0 1015.7 jit_solution(800403736796422366)
XLA Ops:
  7.3 1.8 convert_reduce_fusion
  9.0 1.8 fusion.36
  20.1 2.0 fusion.69
  22.0 35.8 %all-gather.7.cloned.1.call-done = bf16[1,1376,1024]{2,1,0:T(8,128)(2,1)} async-done(((bf16[1,688,1024]{2,1,0:T(8,128)(2,1)}), bf16[1,1376,1024]{2,1,0:T(8,128)(2,1)}) %all-gather.7.cloned.1.call-update) | async-done | bytes 2818064 | tf_op jit(solution)/shard_map/all_gather | solution.py:126
  57.8 2.7 fusion.60
  62.9 5.6 fusion.23
  68.5 2.1 fusion.115
  70.6 2.6 copy.58
  73.2 2.5 copy.57
  75.7 2.5 copy.56
  78.2 25.8 %fusion.116 = (f32[8,1376]{1,0:T(8,128)S(1)}, f32[8,1376,1376]{1,2,0:T(8,128)}) fusion(bf16[1376,8,64]{0,2,1:T(8,128)(2,1)} %bitcast.204, bf16[1376,8,64]{0,2,1:T(8,128)(2,1)} %bitcast.202, pred[1376]{0:T(1024)(128)(4,1)S(1)} %iota_compare_fusion), kind=kOutput, calls=%fused_computation.176 | convolution fusion | flops 1984247040 | bytes 63451488 | tf_op jit(solution)/shard_map/while/body/eval_jaxpr/qhe,khe->hqk/dot_general | solution.py:14
  104.1 23.7 %fusion.1 = f32[8,1376]{1,0:T(8,128)S(1)} fusion(f32[8,1376,1376]{1,2,0:T(8,128)} %get-tuple-element.63, f32[8,1376]{1,0:T(8,128)S(1)} %get-tuple-element.62), kind=kLoop, calls=%fused_computation.7 | loop fusion | flops 30283008 | bytes 60676096 | tf_op jit(solution)/shard_map/while/body/eval_jaxpr/reduce_sum | solution.py:147
  127.8 24.5 %fusion.35 = bf16[8,64,1376]{2,1,0:T(8,128)(2,1)} fusion(bf16[1376,8,64]{0,2,1:T(8,128)(2,1)} %bitcast.214, f32[8,1376,1376]{1,2,0:T(8,128)} %get-tuple-element.63, f32[8,1376]{1,0:T(8,128)S(1)} %fusion.1, f32[8,1376]{1,0:T(8,128)S(1)} %get-tuple-element.62), kind=kOutput, calls=%fused_computation.61 | convolution fusion | flops 1984962560 | bytes 63494144 | tf_op jit(solution)/shard_map/while/body/eval_jaxpr/hqk,khe->qhe/dot_general | solution.py:14
  152.3 1.7 fusion.84
  154.0 3.4 fusion.117
  157.4 5.2 add_bitcast_fusion
  164.6 1.8 fusion.73
  166.5 2.5 convolution_convert_fusion.1
  169.0 11.0 %fusion.67 = bf16[1,4096,16]{0,1,2:T(8,128)(2,1)} fusion(bf16[8,4096,16]{1,2,0:T(8,128)(2,1)} %all-gather.11.cloned.1.call-done, s32[]{:T(128)} %bitcast.198), kind=kOutput, calls=%fused_computation.100 | convolution fusion | flops 1048584 | bytes 1179652 | tf_op jit(solution)/shard_map/sn,n...->s.../dot_general | solution.py:14
  180.0 13.3 %copy.80 = bf16[1,4096,16]{1,2,0:T(8,128)(2,1)S(1)} copy(bf16[1,4096,16]{0,1,2:T(8,128)(2,1)} %fusion.67) | data formatting | bytes 262144 | tf_op jit(solution)/shard_map/sn,n...->s.../dot_general | solution.py:14
  193.3 2.5 fusion.65
  197.3 11.8 %all-gather.13.cloned.1.call-done = bf16[4096,1024]{1,0:T(8,128)(2,1)} async-done(((bf16[2048,1024]{1,0:T(8,128)(2,1)}), bf16[4096,1024]{1,0:T(8,128)(2,1)}) %all-gather.13.cloned.1.call-update) | async-done | bytes 8388624 | tf_op jit(solution)/shard_map/all_gather | solution.py:162
  209.0 11.4 %fusion.108 = f32[688,4096]{1,0:T(8,128)} fusion(bf16[4096,1024]{1,0:T(8,128)(2,1)} %all-gather.13.cloned.1.call-done, bf16[1,688,1024]{2,1,0:T(8,128)(2,1)} %param.21, f32[1024]{0:T(1024)S(1)} %copy-done.73, f32[688]{0:T(1024)S(1)} %fusion.85), kind=kOutput, calls=%fused_computation.169 | convolution fusion | flops 5774180352 | bytes 21076672 | tf_op jit(solution)/shard_map/std,hd->sth/dot_general | solution.py:14
  220.4 60.7 %reduce-scatter.3.cloned.1.call-done = f32[1,688,1024]{2,1,0:T(8,128)} async-done(((f32[1,1376,1024]{2,1,0:T(8,128)}), f32[1,688,1024]{2,1,0:T(8,128)}) %reduce-scatter.3.cloned.1.call-update) | async-done | bytes 2818064 | tf_op jit(solution)/shard_map/reduce_scatter | solution.py:157
  281.2 2.6 fusion.114
  287.5 99.1 %all-gather.9.cloned.1.call-done = bf16[1024,4096]{1,0:T(8,128)(2,1)} async-done(((bf16[1024,2048]{1,0:T(8,128)(2,1)}), bf16[1024,4096]{1,0:T(8,128)(2,1)}) %all-gather.9.cloned.1.call-update) | async-done | bytes 8388624 | tf_op jit(solution)/shard_map/all_gather | solution.py:161
  386.7 8.8 fusion.118
  395.5 28.7 %fusion.9 = (bf16[688,4096]{1,0:T(8,128)(2,1)S(1)}, f32[688,4096]{1,0:T(8,128)}) fusion(f32[688,4096]{1,0:T(8,128)S(1)} %fusion.118, bf16[688,16]{0,1:T(8,128)(2,1)S(1)} %copy-done.54, bf16[1,4096,16]{1,2,0:T(8,128)(2,1)S(1)} %copy.80), kind=kOutput, calls=%fused_computation.16 | convolution fusion | flops 276168704 | bytes 28333568 | tf_op jit(solution)/shard_map/str,shr->sth/dot_general | solution.py:14
  426.6 9.9 fusion.15
  439.0 8.6 fusion.120
  447.6 2.0 fusion.46
  451.9 1.7 multiply_convert_fusion.1
  453.9 2.0 fusion.122
  455.9 3.4 fusion.123
  459.3 4.1 fusion.124
  465.0 1.6 broadcast_multiply_fusion
  466.6 28.4 %all-gather.17.cloned.1.call-done = bf16[1,1376,1024]{2,1,0:T(8,128)(2,1)} async-done(((bf16[1,688,1024]{2,1,0:T(8,128)(2,1)}), bf16[1,1376,1024]{2,1,0:T(8,128)(2,1)}) %all-gather.17.cloned.1.call-update) | async-done | bytes 2818064 | tf_op jit(solution)/shard_map/all_gather | solution.py:190
  495.0 2.8 fusion.57
  497.9 2.9 fusion.44
  500.8 1.6 fusion.32
  502.5 2.5 copy.60
  505.0 23.3 %fusion.29 = bf16[8,64,1376]{2,1,0:T(8,128)(2,1)} fusion(bf16[1376,8,64]{0,2,1:T(8,128)(2,1)} %bitcast.206, f32[8,1376,1376]{1,2,0:T(8,128)} %get-tuple-element.63, f32[8,1376]{1,0:T(8,128)S(1)} %copy-done.14), kind=kOutput, calls=%fused_computation.57 | convolution fusion | flops 1969815552 | bytes 63450112 | tf_op jit(solution)/shard_map/while/body/eval_jaxpr/hqk,qhe->khe/dot_general | solution.py:14
  528.3 43.5 %multiply_reduce_fusion = (f32[8,1376]{1,0:T(8,128)S(1)}, f32[8,1376,1376]{1,2,0:T(8,128)}) fusion(f32[8,1376,1376]{1,2,0:T(8,128)} %get-tuple-element.63, f32[8,1376]{1,0:T(8,128)S(1)} %copy-done.14, bf16[1376,8,64]{0,2,1:T(8,128)(2,1)} %bitcast.207, bf16[1376,8,64]{0,2,1:T(8,128)(2,1)} %bitcast.215), kind=kOutput, calls=%fused_computation.3 | convolution fusion | flops 1984247040 | bytes 124082176 | tf_op jit(solution)/shard_map/while/body/eval_jaxpr/qhe,khe->hqk/dot_general | solution.py:14
  571.8 49.0 %multiply_convert_fusion = bf16[8,1376,1376]{1,2,0:T(8,128)(2,1)} fusion(f32[8,1376,1376]{1,2,0:T(8,128)} %get-tuple-element.69, f32[8,1376,1376]{1,2,0:T(8,128)} %get-tuple-element.63, f32[8,1376]{1,0:T(8,128)S(1)} %get-tuple-element.68, f32[8,1376]{1,0:T(8,128)S(1)} %copy-done.14), kind=kLoop, calls=%fused_computation.2 | loop fusion | flops 60588032 | bytes 151558144 | tf_op jit(solution)/shard_map/while/body/eval_jaxpr/convert_element_type | solution.py:212
  620.8 16.5 %fusion.34 = bf16[8,64,1376]{2,1,0:T(8,128)(2,1)} fusion(bf16[1376,8,64]{0,2,1:T(8,128)(2,1)} %bitcast.205, bf16[8,1376,1376]{1,2,0:T(8,128)(2,1)} %multiply_convert_fusion), kind=kOutput, calls=%fused_computation.60 | convolution fusion | flops 1940226048 | bytes 33112064 | tf_op jit(solution)/shard_map/while/body/eval_jaxpr/hqk,qhe->khe/dot_general | solution.py:14
  637.4 16.5 %fusion.33 = bf16[8,64,1376]{2,1,0:T(8,128)(2,1)} fusion(bf16[1376,8,64]{0,2,1:T(8,128)(2,1)} %bitcast.203, bf16[8,1376,1376]{1,2,0:T(8,128)(2,1)} %multiply_convert_fusion), kind=kOutput, calls=%fused_computation.59 | convolution fusion | flops 1940226048 | bytes 33112064 | tf_op jit(solution)/shard_map/while/body/eval_jaxpr/hqk,khe->qhe/dot_general | solution.py:14
  653.9 2.6 copy.66
  656.5 2.6 copy.64
  659.1 2.6 copy.65
  661.7 3.1 fusion.40
  666.0 2.6 convolution_bitcast_fusion
  671.1 6.3 fusion.111
  677.4 5.0 fusion.24
  682.5 10.7 %fusion.119 = f32[688,1024]{1,0:T(8,128)S(1)} fusion(bf16[688,4096]{1,0:T(8,128)(2,1)} %copy-done.9, bf16[4096,1024]{1,0:T(8,128)(2,1)} %all-gather.13.cloned.1.call-done), kind=kOutput, calls=%fused_computation.179 | convolution fusion | flops 5771362304 | bytes 16842752 | tf_op jit(solution)/shard_map/sth,hd->std/dot_general | solution.py:14
  693.4 2.9 fusion.48
  699.4 130.8 %all-reduce.5.cloned.1.call-done = (f32[8,16,1024]{2,1,0:T(8,128)}, f32[8,1024,16]{1,2,0:T(8,128)}, f32[8,16,1024]{2,1,0:T(8,128)}, f32[8,4096,16]{1,2,0:T(8,128...) async-done(((f32[8,16,1024]{2,1,0:T(8,128)}, f32[8,1024,16]{1,2,0:T(8,128)}, f32[8,16,1024]{2,1,0:T(8,128)}, f32[8,4096,16]{1,2,0:T(8,128)}, f32[8,16,4096]{2,1,0:T(8,128)}, ...) | async-done | bytes 6291472 | tf_op jit(solution)/shard_map/psum | solution.py:237
  830.2 2.4 constant_dynamic-slice_fusion.1
  833.7 68.8 %reduce-scatter.5.cloned.1.call-done = f32[1,688,1024]{2,1,0:T(8,128)} async-done(((f32[1,1376,1024]{2,1,0:T(8,128)}), f32[1,688,1024]{2,1,0:T(8,128)}) %reduce-scatter.5.cloned.1.call-update) | async-done | bytes 2818064 | tf_op jit(solution)/shard_map/reduce_scatter | solution.py:228
  902.6 3.0 fusion.39
  907.9 2.6 add_add_fusion.2
  910.5 89.8 %all-reduce.7.cloned.1.call-done = (f32[8,3,512,16]{2,3,1,0:T(8,128)}, f32[8,16,512]{2,1,0:T(8,128)}) async-done(((f32[8,3,512,16]{2,3,1,0:T(8,128)}, f32[8,16,512]{2,1,0:T(8,128)}), (f32[8,3,512,16]{2,3,1,0:T(8,128)}, f32[8,16,512]{2,1,0:T(8,128)})) %all-reduce.7.cloned.1.call-update) | async-done | bytes 1048592 | tf_op jit(solution)/shard_map/psum | solution.py:236
  1000.3 2.0 copy.131
  1002.3 2.1 copy.132
  1004.4 1.7 copy.133
  (214 shorter events, 39.0 us)
Async XLA Ops:
  7.2 55.3 %copy-start = (bf16[1024,3,512]{2,0,1:T(8,128)(2,1)S(1)}, bf16[1024,3,512]{2,0,1:T(8,128)(2,1)}, u32[]{:S(2)}) copy-start(bf16[1024,3,512]{2,0,1:T(8,128)(2,1)} %param.28) | copy-start | bytes 9437188
  7.2 4.9 copy-start.56
  7.2 50.6 %all-gather.7.cloned.1.call-start = ((), (), s32[]{:S(2)}) async-start(), calls=%async_computation.2 | async-start | bytes 4227072 | tf_op jit(solution)/shard_map/all_gather | solution.py:126
  7.2 4.9 copy-start.4
  13.7 3.4 copy-start.41
  13.7 155.3 %all-gather.11.cloned.1.call-start = ((), (), s32[]{:S(2)}) async-start(), calls=%async_computation.5 | async-start | bytes 1572864 | tf_op jit(solution)/shard_map/all_gather | solution.py:163
  14.5 178.8 %all-gather.15.cloned.1.call-start = ((), (), s32[]{:S(2)}) async-start(), calls=%async_computation.7 | async-start | bytes 1572864 | tf_op jit(solution)/shard_map/all_gather | solution.py:164
  15.2 193.8 %all-gather.13.cloned.1.call-start = ((), (), s32[]{:S(2)}) async-start(), calls=%async_computation.6 | async-start | bytes 12582912 | tf_op jit(solution)/shard_map/all_gather | solution.py:162
  15.8 265.4 %reduce-scatter.3.cloned.1.call-start = ((), (), s32[]{:S(2)}) async-start(), calls=%async_computation.3 | async-start | bytes 8454144 | tf_op jit(solution)/shard_map/reduce_scatter | solution.py:157
  17.6 139.8 %copy-start.19 = (bf16[1,1024,16]{2,1,0:T(8,128)(2,1)}, bf16[1,1024,16]{2,1,0:T(8,128)(2,1)S(1)}, u32[]{:S(2)}) copy-start(bf16[1,1024,16]{2,1,0:T(8,128)(2,1)S(1)} %copy.76) | copy-start | bytes 98308
  18.8 133.5 %copy-start.52 = (bf16[1,16,512]{2,0,1:T(2,128)(2,1)}, bf16[1,16,512]{2,0,1:T(2,128)(2,1)S(1)}, u32[]{:S(2)}) copy-start(bf16[1,16,512]{2,0,1:T(2,128)(2,1)S(1)} %fusion.79) | copy-start | bytes 49156
  20.0 40.4 %copy-start.37 = (bf16[1,16,1024]{2,0,1:T(2,128)(2,1)}, bf16[1,16,1024]{2,0,1:T(2,128)(2,1)S(1)}, u32[]{:S(2)}) copy-start(bf16[1,16,1024]{2,0,1:T(2,128)(2,1)S(1)} %fusion.77) | copy-start | bytes 98308
  57.8 3.3 copy-start.43
  104.1 23.7 %copy-start.34 = (f32[8,1376]{1,0:T(8,128)}, f32[8,1376]{1,0:T(8,128)S(1)}, u32[]{:S(2)}) copy-start(f32[8,1376]{1,0:T(8,128)S(1)} %get-tuple-element.62) | copy-start | bytes 132100
  127.8 24.5 %copy-start.47 = (f32[8,1376]{1,0:T(8,128)}, f32[8,1376]{1,0:T(8,128)S(1)}, u32[]{:S(2)}) copy-start(f32[8,1376]{1,0:T(8,128)S(1)} %fusion.1) | copy-start | bytes 132100
  154.0 3.4 copy-start.28
  162.6 3.9 copy-start.73
  162.6 224.1 %all-gather.9.cloned.1.call-start = ((), (), s32[]{:S(2)}) async-start(), calls=%async_computation.4 | async-start | bytes 12582912 | tf_op jit(solution)/shard_map/all_gather | solution.py:161
  163.2 331.8 %all-gather.17.cloned.1.call-start = ((), (), s32[]{:S(2)}) async-start(), calls=%async_computation.8 | async-start | bytes 4227072 | tf_op jit(solution)/shard_map/all_gather | solution.py:190
  164.0 16.0 %copy-start.26 = (bf16[1,1024,16]{2,1,0:T(8,128)(2,1)}, bf16[1,1024,16]{2,1,0:T(8,128)(2,1)S(1)}, u32[]{:S(2)}) copy-start(bf16[1,1024,16]{2,1,0:T(8,128)(2,1)S(1)} %copy.84) | copy-start | bytes 98308
  164.6 287.2 %copy-start.58 = (f32[688]{0:T(1024)}, f32[688]{0:T(1024)S(1)}, u32[]{:S(2)}) copy-start(f32[688]{0:T(1024)S(1)} %fusion.85) | copy-start | bytes 8260
  197.3 83.9 %copy-start.71 = (f32[1024]{0:T(1024)S(1)}, f32[1024]{0:T(1024)}, u32[]{:S(2)}) copy-start(f32[1024]{0:T(1024)} %param.26) | copy-start | bytes 12292
  386.7 8.8 copy-start.54
  426.6 23.8 %copy-start.45 = (f32[688,16]{0,1:T(8,128)}, f32[688,16]{0,1:T(8,128)S(1)}, u32[]{:S(2)}) copy-start(f32[688,16]{0,1:T(8,128)S(1)} %fusion.82) | copy-start | bytes 132100
  439.0 8.6 copy-start.2
  439.0 8.6 copy-start.40
  439.0 8.6 copy-start.70
  450.9 2.7 copy-start.62
  453.6 376.6 %all-reduce.5.cloned.1.call-start = ((), (), s32[]{:S(2)}) async-start(), calls=%async_computation.10 | async-start | bytes 12582912 | tf_op jit(solution)/shard_map/psum | solution.py:237
  455.9 3.5 copy-start.55
  459.3 4.1 copy-start.68
  463.5 31.6 %copy-start.20 = (bf16[1,1024,16]{2,1,0:T(8,128)(2,1)S(1)}, bf16[1,1024,16]{2,1,0:T(8,128)(2,1)}, u32[]{:S(2)}) copy-start(bf16[1,1024,16]{2,1,0:T(8,128)(2,1)} %copy-done.19) | copy-start | bytes 98308
  495.0 2.8 copy-start.15
  497.8 3.0 copy-start.35
  497.8 3.0 copy-start.53
  500.8 4.2 copy-start.14
  656.5 5.2 copy-start.29
  659.1 6.9 copy-start.44
  661.7 4.3 copy-start.21
  661.7 4.3 copy-start.23
  666.0 2.6 copy-start.12
  671.0 6.4 copy-start.38
  671.0 231.5 %reduce-scatter.5.cloned.1.call-start = ((), (), s32[]{:S(2)}) async-start(), calls=%async_computation.9 | async-start | bytes 8454144 | tf_op jit(solution)/shard_map/reduce_scatter | solution.py:228
  682.4 317.9 %all-reduce.7.cloned.1.call-start = ((), (), s32[]{:S(2)}) async-start(), calls=%async_computation.11 | async-start | bytes 2097152 | tf_op jit(solution)/shard_map/psum | solution.py:236
  682.5 10.8 %copy-start.3 = (f32[1,688,1024]{2,1,0:T(8,128)S(1)}, f32[1,688,1024]{2,1,0:T(8,128)}, u32[]{:S(2)}) copy-start(f32[1,688,1024]{2,1,0:T(8,128)} %copy-done.1) | copy-start | bytes 8454148
  682.5 10.8 %copy-start.27 = (bf16[1,1024,16]{2,1,0:T(8,128)(2,1)S(1)}, bf16[1,1024,16]{2,1,0:T(8,128)(2,1)}, u32[]{:S(2)}) copy-start(bf16[1,1024,16]{2,1,0:T(8,128)(2,1)} %copy-done.26) | copy-start | bytes 98308
  682.5 10.8 %copy-start.46 = (f32[688,16]{0,1:T(8,128)S(1)}, f32[688,16]{0,1:T(8,128)}, u32[]{:S(2)}) copy-start(f32[688,16]{0,1:T(8,128)} %copy-done.45) | copy-start | bytes 132100
  682.5 10.8 %copy-start.59 = (f32[688]{0:T(1024)S(1)}, f32[688]{0:T(1024)}, u32[]{:S(2)}) copy-start(f32[688]{0:T(1024)} %copy-done.58) | copy-start | bytes 8260
  682.5 10.8 %copy-start.75 = (f32[1024]{0:T(1024)S(1)}, f32[1024]{0:T(1024)}, u32[]{:S(2)}) copy-start(f32[1024]{0:T(1024)} %param.27) | copy-start | bytes 12292
  693.3 3.0 copy-start.16
  693.3 3.0 copy-start.36
  693.3 4.2 copy-start.22
  693.3 4.2 copy-start.24
  693.3 4.2 copy-start.25
  693.3 4.2 copy-start.49
  699.4 203.2 %copy-start.51 = (f32[688]{0:T(1024)S(1)}, f32[688]{0:T(1024)}, u32[]{:S(2)}) copy-start(f32[688]{0:T(1024)} %copy-done.50) | copy-start | bytes 8260
  699.4 203.2 %copy-start.57 = (f32[1024]{0:T(1024)S(1)}, f32[1024]{0:T(1024)}, u32[]{:S(2)}) copy-start(f32[1024]{0:T(1024)} %param.24) | copy-start | bytes 12292
  832.7 72.9 %copy-start.65 = (f32[688]{0:T(1024)S(1)}, f32[688]{0:T(1024)}, u32[]{:S(2)}) copy-start(f32[688]{0:T(1024)} %copy-done.64) | copy-start | bytes 8260
  832.7 73.0 %copy-start.61 = (f32[688]{0:T(1024)S(1)}, f32[688]{0:T(1024)}, u32[]{:S(2)}) copy-start(f32[688]{0:T(1024)} %copy-done.60) | copy-start | bytes 8260
  902.6 3.1 copy-start.5
  902.6 3.5 copy-start.8
  1000.3 5.8 copy-start.33
  1000.3 6.6 copy-start.32
  1000.3 7.4 copy-start.31
  (22 other events, 37.6 us)
Sparse Core Ops, SparseCore 0:
  13.8 43.9 all-gather.6
  59.3 21.2 all-gather.10
  82.2 21.2 all-gather.14
  105.0 103.9 all-gather.12
  211.2 69.9 reduce-scatter.2
  282.6 103.9 all-gather.8
  453.8 41.2 all-gather.16
  671.1 159.0 all-reduce.4
  832.5 69.9 reduce-scatter.4
  907.0 93.2 all-reduce.6
where the time goes:
time: 1020 us
  waiting for transfers between devices  528 us (52%)
  matrix products  317 us (31%)
  other arithmetic  99.8 us (10%)
  local copies, waits for them, and re-layouts  53.6 us (5%)
  between operations  16.7 us (2%)
    dot_general x38, matrix products, product(): return jnp.einsum(form, left, right, preferred_element_type=jnp.float32)  295 us
    psum x1, waiting for transfers between devices, body(): lax.psum((stack_slots(grad_qkv_a), stack_slots(grad_out_b), stack_slots(g...  131 us
    all_gather x1, waiting for transfers between devices, body(): lax.all_gather(w_up, 'tensor', axis=1, tiled=True)  99.1 us
    psum x1, waiting for transfers between devices, body(): lax.psum((stack_slots(grad_qkv_b), stack_slots(grad_out_a)), 'dp')  89.8 us
    reduce_scatter x1, waiting for transfers between devices, body(): lax.psum_scatter(grad_one_terms, 'tensor', scatter_dimension=1, tiled=True)  68.8 us
    reduce_scatter x1, waiting for transfers between devices, body(): lax.psum_scatter(attn_terms, 'tensor', scatter_dimension=1, tiled=True)  60.7 us
    convert_element_type x1, other arithmetic, attend_back(): grad_scores = (soft * (grad_soft - jnp.sum(soft * grad_soft, axis=-1, kee...  49 us
    all_gather x1, waiting for transfers between devices, body(): full_one = lax.all_gather(normed_one, 'tensor', axis=1, tiled=True)  35.8 us
  transfers between devices with their start and end apart: 10, of which 8 were waited for; matrix products, arithmetic and copies ran while one was open for 21% of the time, Pallas kernels for 0%

commit v1 on v0

--- a/solution.py
+++ b/solution.py
@@ -234,17 +234,16 @@
 
     grad_up_a, grad_up_b, grad_down_a, grad_down_b = ffn_grads
     sum_qkv_b, sum_out_a = lax.psum((stack_slots(grad_qkv_b), stack_slots(grad_out_a)), "dp")
-    joint_sums = lax.psum(
-        (
-            stack_slots(grad_qkv_a),
-            stack_slots(grad_out_b),
-            stack_slots(grad_up_a),
-            stack_slots(grad_up_b),
-            stack_slots(grad_down_a),
-            stack_slots(grad_down_b),
-        ),
-        ("dp", "tensor"),
-    )
+    joint_sums = (
+        stack_slots(grad_qkv_a),
+        stack_slots(grad_out_b),
+        stack_slots(grad_up_a),
+        stack_slots(grad_up_b),
+        stack_slots(grad_down_a),
+        stack_slots(grad_down_b),
+    )
+    for mesh_axis in ("tensor", "dp"):
+        joint_sums = lax.psum(joint_sums, mesh_axis)
     sum_qkv_a, sum_out_b, sum_up_a, up_b_whole, down_a_whole, sum_down_b = joint_sums
     width_local = w_up.shape[1]
     first_col = lax.axis_index("tensor") * width_local

time: 1020 us -> 1090 us (1.069)
  waiting for transfers between devices: 528 us -> 583 us
  matrix products: 317 us -> 332 us
    psum x2, waiting for transfers between devices: 221 us -> 287 us  [body(): joint_sums = lax.psum(joint_sums, mesh_axis)]
    dot_general x38, matrix products: 295 us -> 309 us  [product(): return jnp.einsum(form, left, right, preferred_element_type=jnp.float32)]
    all_gather x1, waiting for transfers between devices: 11.8 us -> 0.8 us  [body(): lax.all_gather(w_down, 'tensor', axis=0, tiled=True)]
  transfers between devices with their start and end apart: 10 -> 10, of which waited for: 8 -> 8; matrix products, arithmetic and copies ran while one was open for 21% -> 20% of each run, Pallas kernels for 0% -> 0%
where the time goes in v1:
time: 1090 us; the launch traced here: 1080 us
  waiting for transfers between devices  583 us (53%)
  matrix products  332 us (30%)
  other arithmetic  99.8 us (9%)
  local copies, waits for them, and re-layouts  50 us (5%)
  between operations  16.6 us (2%)
    dot_general x38, matrix products, product(): return jnp.einsum(form, left, right, preferred_element_type=jnp.float32)  309 us
    psum x2, waiting for transfers between devices, body(): joint_sums = lax.psum(joint_sums, mesh_axis)  287 us
    all_gather x1, waiting for transfers between devices, body(): lax.all_gather(w_up, 'tensor', axis=1, tiled=True)  99.1 us
    reduce_scatter x1, waiting for transfers between devices, body(): lax.psum_scatter(grad_one_terms, 'tensor', scatter_dimension=1, tiled=True)  68.7 us
    reduce_scatter x1, waiting for transfers between devices, body(): lax.psum_scatter(attn_terms, 'tensor', scatter_dimension=1, tiled=True)  60.7 us
    convert_element_type x1, other arithmetic, attend_back(): grad_scores = (soft * (grad_soft - jnp.sum(soft * grad_soft, axis=-1, kee...  49 us
    all_gather x1, waiting for transfers between devices, body(): full_one = lax.all_gather(normed_one, 'tensor', axis=1, tiled=True)  35.8 us
    all_gather x1, waiting for transfers between devices, body(): full_grad_attn = lax.all_gather(grad_attn, 'tensor', axis=1, tiled=True)  28.4 us
  transfers between devices with their start and end apart: 10, of which 8 were waited for; matrix products, arithmetic and copies ran while one was open for 20% of the time, Pallas kernels for 0%

profile of v1, /device:TPU:0, one launch (start us, length us, event | category | flops | bytes accessed | tf_op | source)
XLA Modules:
  0.0 1082.3 jit_solution(14175524826322393596)
XLA Ops:
  7.3 1.8 convert_reduce_fusion
  9.0 1.8 fusion.36
  12.1 1.6 fusion.38
  20.0 2.0 fusion.69
  22.0 35.8 %all-gather.7.cloned.1.call-done = bf16[1,1376,1024]{2,1,0:T(8,128)(2,1)} async-done(((bf16[1,688,1024]{2,1,0:T(8,128)(2,1)}), bf16[1,1376,1024]{2,1,0:T(8,128)(2,1)}) %all-gather.7.cloned.1.call-update) | async-done | bytes 2818064 | tf_op jit(solution)/shard_map/all_gather | solution.py:126
  57.8 2.7 fusion.60
  62.9 5.4 fusion.23
  68.3 2.1 fusion.115
  70.4 2.6 copy.58
  73.0 2.5 copy.57
  75.5 2.5 copy.56
  78.0 25.8 %fusion.116 = (f32[8,1376]{1,0:T(8,128)S(1)}, f32[8,1376,1376]{1,2,0:T(8,128)}) fusion(bf16[1376,8,64]{0,2,1:T(8,128)(2,1)} %bitcast.204, bf16[1376,8,64]{0,2,1:T(8,128)(2,1)} %bitcast.202, pred[1376]{0:T(1024)(128)(4,1)S(1)} %iota_compare_fusion), kind=kOutput, calls=%fused_computation.176 | convolution fusion | flops 1984247040 | bytes 63451488 | tf_op jit(solution)/shard_map/while/body/eval_jaxpr/qhe,khe->hqk/dot_general | solution.py:14
  103.9 23.7 %fusion.1 = f32[8,1376]{1,0:T(8,128)S(1)} fusion(f32[8,1376,1376]{1,2,0:T(8,128)} %get-tuple-element.69, f32[8,1376]{1,0:T(8,128)S(1)} %get-tuple-element.68), kind=kLoop, calls=%fused_computation.7 | loop fusion | flops 30283008 | bytes 60676096 | tf_op jit(solution)/shard_map/while/body/eval_jaxpr/reduce_sum | solution.py:147
  127.6 35.6 %fusion.35 = bf16[8,64,1376]{2,1,0:T(8,128)(2,1)} fusion(bf16[1376,8,64]{0,2,1:T(8,128)(2,1)} %bitcast.214, f32[8,1376,1376]{1,2,0:T(8,128)} %get-tuple-element.69, f32[8,1376]{1,0:T(8,128)S(1)} %fusion.1, f32[8,1376]{1,0:T(8,128)S(1)} %get-tuple-element.68), kind=kOutput, calls=%fused_computation.61 | convolution fusion | flops 1984962560 | bytes 63494144 | tf_op jit(solution)/shard_map/while/body/eval_jaxpr/hqk,khe->qhe/dot_general | solution.py:14
  163.2 1.7 fusion.84
  164.9 3.4 fusion.117
  168.3 5.2 add_bitcast_fusion
  175.5 1.8 fusion.73
  177.4 2.5 convolution_convert_fusion.1
  179.9 11.0 %fusion.67 = bf16[1,4096,16]{0,1,2:T(8,128)(2,1)} fusion(bf16[8,4096,16]{1,2,0:T(8,128)(2,1)} %all-gather.11.cloned.1.call-done, s32[]{:T(128)} %bitcast.198), kind=kOutput, calls=%fused_computation.100 | convolution fusion | flops 1048584 | bytes 1179652 | tf_op jit(solution)/shard_map/sn,n...->s.../dot_general | solution.py:14
  190.9 13.3 %copy.80 = bf16[1,4096,16]{1,2,0:T(8,128)(2,1)S(1)} copy(bf16[1,4096,16]{0,1,2:T(8,128)(2,1)} %fusion.67) | data formatting | bytes 262144 | tf_op jit(solution)/shard_map/sn,n...->s.../dot_general | solution.py:14
  204.2 2.5 fusion.65
  209.0 11.4 %fusion.108 = f32[688,4096]{1,0:T(8,128)} fusion(bf16[4096,1024]{1,0:T(8,128)(2,1)} %all-gather.13.cloned.1.call-done, bf16[1,688,1024]{2,1,0:T(8,128)(2,1)} %param.21, f32[1024]{0:T(1024)S(1)} %copy-done.71, f32[688]{0:T(1024)S(1)} %fusion.85), kind=kOutput, calls=%fused_computation.169 | convolution fusion | flops 5774180352 | bytes 21076672 | tf_op jit(solution)/shard_map/std,hd->sth/dot_general | solution.py:14
  220.4 60.7 %reduce-scatter.3.cloned.1.call-done = f32[1,688,1024]{2,1,0:T(8,128)} async-done(((f32[1,1376,1024]{2,1,0:T(8,128)}), f32[1,688,1024]{2,1,0:T(8,128)}) %reduce-scatter.3.cloned.1.call-update) | async-done | bytes 2818064 | tf_op jit(solution)/shard_map/reduce_scatter | solution.py:157
  281.1 2.6 fusion.114
  287.5 99.1 %all-gather.9.cloned.1.call-done = bf16[1024,4096]{1,0:T(8,128)(2,1)} async-done(((bf16[1024,2048]{1,0:T(8,128)(2,1)}), bf16[1024,4096]{1,0:T(8,128)(2,1)}) %all-gather.9.cloned.1.call-update) | async-done | bytes 8388624 | tf_op jit(solution)/shard_map/all_gather | solution.py:161
  386.7 8.8 fusion.118
  395.5 28.7 %fusion.9 = (bf16[688,4096]{1,0:T(8,128)(2,1)S(1)}, f32[688,4096]{1,0:T(8,128)}) fusion(f32[688,4096]{1,0:T(8,128)S(1)} %fusion.118, bf16[688,16]{0,1:T(8,128)(2,1)S(1)} %copy-done.51, bf16[1,4096,16]{1,2,0:T(8,128)(2,1)S(1)} %copy.80), kind=kOutput, calls=%fused_computation.16 | convolution fusion | flops 276168704 | bytes 28333568 | tf_op jit(solution)/shard_map/str,shr->sth/dot_general | solution.py:14
  426.5 10.0 fusion.15
  438.9 8.6 fusion.120
  447.5 2.0 fusion.46
  452.4 1.7 multiply_convert_fusion.1
  454.4 2.0 fusion.122
  456.4 3.5 fusion.123
  459.9 4.1 fusion.124
  464.0 1.6 broadcast_multiply_fusion.1
  465.5 1.6 broadcast_multiply_fusion
  467.1 28.4 %all-gather.17.cloned.1.call-done = bf16[1,1376,1024]{2,1,0:T(8,128)(2,1)} async-done(((bf16[1,688,1024]{2,1,0:T(8,128)(2,1)}), bf16[1,1376,1024]{2,1,0:T(8,128)(2,1)}) %all-gather.17.cloned.1.call-update) | async-done | bytes 2818064 | tf_op jit(solution)/shard_map/all_gather | solution.py:190
  495.6 2.8 fusion.57
  498.3 2.9 fusion.44
  501.3 1.6 fusion.32
  502.9 2.6 copy.60
  505.5 23.2 %fusion.29 = bf16[8,64,1376]{2,1,0:T(8,128)(2,1)} fusion(bf16[1376,8,64]{0,2,1:T(8,128)(2,1)} %bitcast.206, f32[8,1376,1376]{1,2,0:T(8,128)} %get-tuple-element.69, f32[8,1376]{1,0:T(8,128)S(1)} %copy-done.14), kind=kOutput, calls=%fused_computation.57 | convolution fusion | flops 1969815552 | bytes 63450112 | tf_op jit(solution)/shard_map/while/body/eval_jaxpr/hqk,qhe->khe/dot_general | solution.py:14
  528.7 43.6 %multiply_reduce_fusion = (f32[8,1376]{1,0:T(8,128)S(1)}, f32[8,1376,1376]{1,2,0:T(8,128)}) fusion(f32[8,1376,1376]{1,2,0:T(8,128)} %get-tuple-element.69, f32[8,1376]{1,0:T(8,128)S(1)} %copy-done.14, bf16[1376,8,64]{0,2,1:T(8,128)(2,1)} %bitcast.207, bf16[1376,8,64]{0,2,1:T(8,128)(2,1)} %bitcast.215), kind=kOutput, calls=%fused_computation.3 | convolution fusion | flops 1984247040 | bytes 124082176 | tf_op jit(solution)/shard_map/while/body/eval_jaxpr/qhe,khe->hqk/dot_general | solution.py:14
  572.2 49.0 %multiply_convert_fusion = bf16[8,1376,1376]{1,2,0:T(8,128)(2,1)} fusion(f32[8,1376,1376]{1,2,0:T(8,128)} %get-tuple-element.75, f32[8,1376,1376]{1,2,0:T(8,128)} %get-tuple-element.69, f32[8,1376]{1,0:T(8,128)S(1)} %get-tuple-element.74, f32[8,1376]{1,0:T(8,128)S(1)} %copy-done.14), kind=kLoop, calls=%fused_computation.2 | loop fusion | flops 60588032 | bytes 151558144 | tf_op jit(solution)/shard_map/while/body/eval_jaxpr/convert_element_type | solution.py:212
  621.2 16.6 %fusion.34 = bf16[8,64,1376]{2,1,0:T(8,128)(2,1)} fusion(bf16[1376,8,64]{0,2,1:T(8,128)(2,1)} %bitcast.205, bf16[8,1376,1376]{1,2,0:T(8,128)(2,1)} %multiply_convert_fusion), kind=kOutput, calls=%fused_computation.60 | convolution fusion | flops 1940226048 | bytes 33112064 | tf_op jit(solution)/shard_map/while/body/eval_jaxpr/hqk,qhe->khe/dot_general | solution.py:14
  637.8 16.5 %fusion.33 = bf16[8,64,1376]{2,1,0:T(8,128)(2,1)} fusion(bf16[1376,8,64]{0,2,1:T(8,128)(2,1)} %bitcast.203, bf16[8,1376,1376]{1,2,0:T(8,128)(2,1)} %multiply_convert_fusion), kind=kOutput, calls=%fused_computation.59 | convolution fusion | flops 1940226048 | bytes 33112064 | tf_op jit(solution)/shard_map/while/body/eval_jaxpr/hqk,khe->qhe/dot_general | solution.py:14
  654.3 2.5 copy.66
  656.8 2.6 copy.64
  659.4 2.5 copy.65
  662.0 3.1 fusion.40
  666.3 2.6 convolution_bitcast_fusion
  671.4 1.8 fusion.121
  674.0 2.6 fusion.110
  677.6 148.9 %all-reduce.7.cloned.1.call-done = (f32[8,16,1024]{2,1,0:T(8,128)}, f32[8,1024,16]{1,2,0:T(8,128)}, f32[8,16,1024]{2,1,0:T(8,128)}, f32[8,4096,16]{1,2,0:T(8,128...) async-done(((f32[8,16,1024]{2,1,0:T(8,128)}, f32[8,1024,16]{1,2,0:T(8,128)}, f32[8,16,1024]{2,1,0:T(8,128)}, f32[8,4096,16]{1,2,0:T(8,128)}, f32[8,16,4096]{2,1,0:T(8,128)}, ...) | async-done | bytes 6291472 | tf_op jit(solution)/shard_map/psum | solution.py:246
  826.7 6.6 fusion.111
  833.2 5.0 fusion.24
  838.3 10.4 fusion.119
  848.8 2.9 fusion.48
  851.7 138.4 %all-reduce.5.cloned.1.call-done = (f32[8,16,1024]{2,1,0:T(8,128)}, f32[8,3,512,16]{2,3,1,0:T(8,128)}, f32[8,16,512]{2,1,0:T(8,128)}, f32[8,1024,16]{1,2,0:T(8,1...) async-done(((f32[8,16,1024]{2,1,0:T(8,128)}, f32[8,3,512,16]{2,3,1,0:T(8,128)}, ...) | async-done | bytes 7340048 | tf_op jit(solution)/shard_map/psum | solution.py:246
  990.1 2.4 constant_dynamic-slice_fusion.1
  993.6 68.7 %reduce-scatter.5.cloned.1.call-done = f32[1,688,1024]{2,1,0:T(8,128)} async-done(((f32[1,1376,1024]{2,1,0:T(8,128)}), f32[1,688,1024]{2,1,0:T(8,128)}) %reduce-scatter.5.cloned.1.call-update) | async-done | bytes 2818064 | tf_op jit(solution)/shard_map/reduce_scatter | solution.py:228
  1062.3 3.0 fusion.39
  1067.6 2.6 add_add_fusion.2
  (210 shorter events, 38.2 us)
Async XLA Ops:
  7.2 55.2 %copy-start = (bf16[1024,3,512]{2,0,1:T(8,128)(2,1)S(1)}, bf16[1024,3,512]{2,0,1:T(8,128)(2,1)}, u32[]{:S(2)}) copy-start(bf16[1024,3,512]{2,0,1:T(8,128)(2,1)} %param.28) | copy-start | bytes 9437188
  7.2 4.9 copy-start.53
  7.2 50.6 %all-gather.7.cloned.1.call-start = ((), (), s32[]{:S(2)}) async-start(), calls=%async_computation.2 | async-start | bytes 4227072 | tf_op jit(solution)/shard_map/all_gather | solution.py:126
  7.2 4.8 copy-start.4
  9.0 2.5 copy-start.47
  13.7 3.4 copy-start.37
  13.7 166.2 %all-gather.11.cloned.1.call-start = ((), (), s32[]{:S(2)}) async-start(), calls=%async_computation.5 | async-start | bytes 1572864 | tf_op jit(solution)/shard_map/all_gather | solution.py:163
  14.5 189.8 %all-gather.15.cloned.1.call-start = ((), (), s32[]{:S(2)}) async-start(), calls=%async_computation.7 | async-start | bytes 1572864 | tf_op jit(solution)/shard_map/all_gather | solution.py:164
  15.2 193.8 %all-gather.13.cloned.1.call-start = ((), (), s32[]{:S(2)}) async-start(), calls=%async_computation.6 | async-start | bytes 12582912 | tf_op jit(solution)/shard_map/all_gather | solution.py:162
  15.8 265.4 %reduce-scatter.3.cloned.1.call-start = ((), (), s32[]{:S(2)}) async-start(), calls=%async_computation.3 | async-start | bytes 8454144 | tf_op jit(solution)/shard_map/reduce_scatter | solution.py:157
  17.6 150.7 %copy-start.18 = (bf16[1,1024,16]{2,1,0:T(8,128)(2,1)}, bf16[1,1024,16]{2,1,0:T(8,128)(2,1)S(1)}, u32[]{:S(2)}) copy-start(bf16[1,1024,16]{2,1,0:T(8,128)(2,1)S(1)} %copy.76) | copy-start | bytes 98308
  18.8 144.4 %copy-start.49 = (bf16[1,16,512]{2,0,1:T(2,128)(2,1)}, bf16[1,16,512]{2,0,1:T(2,128)(2,1)S(1)}, u32[]{:S(2)}) copy-start(bf16[1,16,512]{2,0,1:T(2,128)(2,1)S(1)} %fusion.79) | copy-start | bytes 49156
  20.0 40.4 %copy-start.33 = (bf16[1,16,1024]{2,0,1:T(2,128)(2,1)}, bf16[1,16,1024]{2,0,1:T(2,128)(2,1)S(1)}, u32[]{:S(2)}) copy-start(bf16[1,16,1024]{2,0,1:T(2,128)(2,1)S(1)} %fusion.77) | copy-start | bytes 98308
  57.8 3.3 copy-start.40
  103.9 23.7 %copy-start.32 = (f32[8,1376]{1,0:T(8,128)}, f32[8,1376]{1,0:T(8,128)S(1)}, u32[]{:S(2)}) copy-start(f32[8,1376]{1,0:T(8,128)S(1)} %get-tuple-element.68) | copy-start | bytes 132100
  127.6 35.6 %copy-start.44 = (f32[8,1376]{1,0:T(8,128)}, f32[8,1376]{1,0:T(8,128)S(1)}, u32[]{:S(2)}) copy-start(f32[8,1376]{1,0:T(8,128)S(1)} %fusion.1) | copy-start | bytes 132100
  164.9 3.4 copy-start.24
  173.5 3.9 copy-start.71
  173.5 213.2 %all-gather.9.cloned.1.call-start = ((), (), s32[]{:S(2)}) async-start(), calls=%async_computation.4 | async-start | bytes 12582912 | tf_op jit(solution)/shard_map/all_gather | solution.py:161
  174.1 321.5 %all-gather.17.cloned.1.call-start = ((), (), s32[]{:S(2)}) async-start(), calls=%async_computation.8 | async-start | bytes 4227072 | tf_op jit(solution)/shard_map/all_gather | solution.py:190
  174.9 16.1 %copy-start.22 = (bf16[1,1024,16]{2,1,0:T(8,128)(2,1)}, bf16[1,1024,16]{2,1,0:T(8,128)(2,1)S(1)}, u32[]{:S(2)}) copy-start(bf16[1,1024,16]{2,1,0:T(8,128)(2,1)S(1)} %copy.84) | copy-start | bytes 98308
  175.5 276.9 %copy-start.55 = (f32[688]{0:T(1024)}, f32[688]{0:T(1024)S(1)}, u32[]{:S(2)}) copy-start(f32[688]{0:T(1024)S(1)} %fusion.85) | copy-start | bytes 8260
  208.2 72.9 %copy-start.69 = (f32[1024]{0:T(1024)S(1)}, f32[1024]{0:T(1024)}, u32[]{:S(2)}) copy-start(f32[1024]{0:T(1024)} %param.26) | copy-start | bytes 12292
  386.7 8.8 copy-start.51
  426.5 23.9 %copy-start.42 = (f32[688,16]{0,1:T(8,128)}, f32[688,16]{0,1:T(8,128)S(1)}, u32[]{:S(2)}) copy-start(f32[688,16]{0,1:T(8,128)S(1)} %fusion.82) | copy-start | bytes 132100
  438.9 8.6 copy-start.2
  438.9 8.6 copy-start.36
  438.9 8.6 copy-start.68
  449.6 2.9 copy-start.70
  450.9 3.2 copy-start.60
  454.1 372.4 %all-reduce.7.cloned.1.call-start = ((), (), s32[]{:S(2)}) async-start(), calls=%async_computation.11 | async-start | bytes 12582912 | tf_op jit(solution)/shard_map/psum | solution.py:246
  456.4 3.5 copy-start.52
  459.9 4.1 copy-start.66
  464.0 31.6 %copy-start.19 = (bf16[1,1024,16]{2,1,0:T(8,128)(2,1)S(1)}, bf16[1,1024,16]{2,1,0:T(8,128)(2,1)}, u32[]{:S(2)}) copy-start(bf16[1,1024,16]{2,1,0:T(8,128)(2,1)} %copy-done.18) | copy-start | bytes 98308
  495.6 2.8 copy-start.15
  498.3 2.9 copy-start.50
  501.3 4.2 copy-start.14
  656.8 5.2 copy-start.25
  659.4 6.9 copy-start.41
  662.0 3.2 copy-start.59
  662.0 4.3 copy-start.20
  662.0 4.3 copy-start.21
  666.3 2.6 copy-start.12
  671.3 2.7 copy-start.46
  671.3 318.7 %all-reduce.5.cloned.1.call-start = ((), (), s32[]{:S(2)}) async-start(), calls=%async_computation.10 | async-start | bytes 14680064 | tf_op jit(solution)/shard_map/psum | solution.py:246
  826.6 6.6 copy-start.34
  826.6 235.7 %reduce-scatter.5.cloned.1.call-start = ((), (), s32[]{:S(2)}) async-start(), calls=%async_computation.9 | async-start | bytes 8454144 | tf_op jit(solution)/shard_map/reduce_scatter | solution.py:228
  838.2 10.5 copy-start.3
  838.3 10.5 copy-start.23
  838.3 10.5 copy-start.43
  838.3 10.5 copy-start.56
  838.3 10.5 copy-start.73
  851.7 210.6 %copy-start.48 = (f32[688]{0:T(1024)S(1)}, f32[688]{0:T(1024)}, u32[]{:S(2)}) copy-start(f32[688]{0:T(1024)} %copy-done.47) | copy-start | bytes 8260
  990.1 2.5 copy-start.27
  990.1 72.2 %copy-start.54 = (f32[1024]{0:T(1024)S(1)}, f32[1024]{0:T(1024)}, u32[]{:S(2)}) copy-start(f32[1024]{0:T(1024)} %param.24) | copy-start | bytes 12292
  992.5 72.8 %copy-start.63 = (f32[688]{0:T(1024)S(1)}, f32[688]{0:T(1024)}, u32[]{:S(2)}) copy-start(f32[688]{0:T(1024)} %copy-done.62) | copy-start | bytes 8260
  992.5 72.8 %copy-start.58 = (f32[688]{0:T(1024)S(1)}, f32[688]{0:T(1024)}, u32[]{:S(2)}) copy-start(f32[688]{0:T(1024)} %copy-done.57) | copy-start | bytes 8260
  1062.3 3.1 copy-start.5
  1062.3 3.5 copy-start.8
  1067.6 2.6 copy-start.31
  1067.6 3.4 copy-start.26
  1067.6 4.3 copy-start.39
  1070.2 3.2 copy-start.29
  1070.2 4.0 copy-start.28
  (20 other events, 33.2 us)
Sparse Core Ops, SparseCore 0:
  13.8 43.9 all-gather.6
  59.3 21.2 all-gather.10
  82.2 21.2 all-gather.14
  105.0 103.9 all-gather.12
  211.2 69.9 reduce-scatter.2
  282.6 103.9 all-gather.8
  454.3 41.2 all-gather.16
  671.5 155.0 all-reduce.6
  832.5 157.5 all-reduce.4
  992.3 69.9 reduce-scatter.4
